TPU v7x, 128 devices: a whole 4x4x4 slice. The times are simulated.
128 devices in a mesh: cplx: 4 (over y), frag: 32 (over z, x, core).
Axes of the slice: x: 4, y: 4, z: 4, core: 2. Of those that a mesh axis runs over, the one named last changes fastest.
Arguments:
- coeffs: float32 [2048, 256], P(('cplx', 'frag')), parts along dimension 0, may hold values from -0.3 to 0.3
- centres: float32 [2048, 4, 256], P(('cplx', 'frag')), parts along dimension 0, may hold values from -3 to 3, as said below
- frag_sizes: int32 [2048], P(('cplx', 'frag')), parts along dimension 0, may hold values from 64 to 256
- pairs: int32 [131072, 2], P(('cplx', 'frag')), parts along dimension 0, may hold values from 0 to 511, as said below
Outputs:
- potential: float32 [2048, 256], P(('cplx', 'frag')), parts along dimension 0
There are 4 independent parts, one for each index of `cplx`. A program takes and returns all parts, laid end to end along the dimension named above; each array names one. Nothing has to cross between parts.
Inputs may be any that keep to these rules, and one draw needn't show every extreme that they name: `pairs`: slots 1024 * d to 1024 * (d + 1) - 1 belong to device d of frag; their first fragment is one of fragments 16 * d to 16 * (d + 1) - 1. Slot r of that block (counted from the block's start) either has its second fragment equal to its first (an empty slot) or names a second fragment owned by device r // 32, that is one of fragments 16 * (r // 32) on. Slots toward the device itself are never empty and never name the same fragment twice. `centres`: widths are positive.
All inputs are finite; a program needn't handle non-finite values.
Results may differ from a plain program's by a relative error of at most 0.0003.
Values sent between devices are 32-bit elements; how exact they have to be, the bound alone decides.
No kernel may reach another device: no remote copies, remote signals or barrier semaphores. Data moves between devices by JAX's collectives and lax.ppermute only.
A program may use at most 128 MiB of HBM per device.

v0:
```python
import jax
import jax.numpy as jnp
from jax import lax
from jax.sharding import PartitionSpec as P


def pair_terms(mine, partner):
    delta = (mine[:, 1, :, None] - partner[:, 1, None, :]) ** 2
    delta = delta + (mine[:, 2, :, None] - partner[:, 2, None, :]) ** 2
    delta = delta + (mine[:, 3, :, None] - partner[:, 3, None, :]) ** 2
    kernel = lax.rsqrt(delta + mine[:, 4, :, None] + partner[:, 4, None, :])
    to_first = jnp.sum(kernel * partner[:, 0, None, :], axis=2)
    to_second = jnp.sum(kernel * mine[:, 0, :, None], axis=1)
    return (to_first, to_second)


def run_blocks(mine, partner, live_f, count, row_block):
    slot_total = mine.shape[0]
    width = mine.shape[2]

    def one_block(k, bufs):
        start = k * row_block
        own = lax.dynamic_slice_in_dim(mine, start, row_block, 0)
        other = lax.dynamic_slice_in_dim(partner, start, row_block, 0)
        weight = lax.dynamic_slice_in_dim(live_f, start, row_block, 0)[:, None]
        to_first, to_second = pair_terms(own, other)
        first_buf = lax.dynamic_update_slice_in_dim(bufs[0], to_first * weight, start, 0)
        second_buf = lax.dynamic_update_slice_in_dim(bufs[1], to_second * weight, start, 0)
        return (first_buf, second_buf)

    empty = jnp.zeros((slot_total, width), jnp.float32)
    return lax.fori_loop(0, count, one_block, (empty, empty))


def local(coeffs, centres, frag_sizes, pairs):
    frag_dev, width = coeffs.shape
    slot_total = pairs.shape[0]
    row_block = min(64, slot_total)
    peers = lax.axis_size("frag")
    per_peer = slot_total // peers
    owner = lax.axis_index("frag")
    mask = (jnp.arange(width, dtype=jnp.int32)[None, :] < frag_sizes[:, None]).astype(jnp.float32)
    packed = jnp.concatenate([(coeffs * mask)[:, None, :], centres], axis=1)
    first_local = pairs[:, 0] - owner * frag_dev
    second = pairs[:, 1]
    second_slot = second % frag_dev
    live = pairs[:, 0] != second
    live_f = live.astype(jnp.float32)
    wanted = lax.all_to_all(
        second_slot.reshape(peers, per_peer), "frag", split_axis=0, concat_axis=0, tiled=True
    )
    served = packed[wanted]
    returned = lax.all_to_all(served, "frag", split_axis=0, concat_axis=0, tiled=True)
    partner = returned.reshape(slot_total, 5, width)
    mine = packed[first_local]
    to_first, to_second = run_blocks(mine, partner, live_f, slot_total // row_block, row_block)
    frag_ids = jnp.arange(frag_dev, dtype=jnp.int32)[:, None]
    own_table = (first_local[None, :] == frag_ids).astype(jnp.float32)
    total = jnp.dot(own_table, to_first, precision=lax.Precision.HIGHEST)
    back_values, back_slots = (
        lax.all_to_all(
            to_second.reshape(peers, per_peer, width),
            "frag",
            split_axis=0,
            concat_axis=0,
            tiled=True,
        ),
        lax.all_to_all(
            second_slot.reshape(peers, per_peer), "frag", split_axis=0, concat_axis=0, tiled=True
        ),
    )
    back_table = (back_slots.reshape(1, slot_total) == frag_ids).astype(jnp.float32)
    total = total + jnp.dot(
        back_table, back_values.reshape(slot_total, width), precision=lax.Precision.HIGHEST
    )
    return total * mask


def solution(mesh):
    return jax.shard_map(
        local,
        mesh=mesh,
        in_specs=(
            P(("cplx", "frag"), None),
            P(("cplx", "frag"), None, None),
            P(("cplx", "frag")),
            P(("cplx", "frag"), None),
        ),
        out_specs=P(("cplx", "frag"), None),
        check_vma=False,
    )
```

profile of v0, /device:TPU:0, one launch (start us, length us, event | category | flops | bytes accessed | tf_op | source)
XLA Modules:
  0.0 435.6 jit_solution(4605263056413246346)
XLA Ops:
  1.5 8.2 %all-to-all-start = ((s32[32,1,32]{2,1,0:T(1,128)}), s32[32,1,32]{2,1,0:T(1,128)S(1)}, u32[]{:S(2)}, u32[]{:S(2)}) async-start(s32[32,1,32]{2,1,0:T(1,128)} %and_select_fusion), calls=%async_computation | async-start | bytes 32768 | tf_op jit(solution)/shard_map/all_to_all | solution.py:49
  17.2 10.6 %gather_fusion.1 = f32[1024,5,256]{2,1,0:T(8,128)} fusion(f32[16,5,256]{2,1,0:T(8,128)S(1)} %pad_maximum_fusion, s32[1024]{0:T(1024)S(1)} %broadcast_clamp_fusion), kind=kCustom, calls=%fused_computation.1 | custom fusion | bytes 10489856 | tf_op jit(solution)/shard_map/gather | solution.py:52
  27.7 7.9 %copy.18 = f32[32,32,5,256]{3,1,2,0:T(8,128)} copy(f32[32,32,5,256]{3,2,1,0:T(8,128)} %bitcast.36) | data formatting | bytes 10485760 | tf_op jit(solution)/shard_map/gather | solution.py:52
  40.5 10.6 %gather_fusion = f32[1024,5,256]{2,1,0:T(8,128)} fusion(f32[16,5,256]{2,1,0:T(8,128)S(1)} %pad_maximum_fusion, s32[1024]{0:T(1024)S(1)} %broadcast_clamp_fusion.1), kind=kCustom, calls=%fused_computation | custom fusion | bytes 10489856 | tf_op jit(solution)/shard_map/gather | solution.py:55
  51.1 7.5 %copy.20 = f32[1024,5,256]{2,0,1:T(8,128)} copy(f32[1024,5,256]{2,1,0:T(8,128)} %gather_fusion) | data formatting | bytes 10485760 | tf_op jit(solution)/shard_map/while | solution.py:32
  58.5 47.7 %all-to-all-done.1 = f32[32,32,5,256]{3,1,2,0:T(8,128)} async-done(((f32[32,32,5,256]{3,1,2,0:T(8,128)}), f32[32,32,5,256]{3,1,2,0:T(8,128)}, u32[]{:S(2)}, u32[]{:S(2)}) %all-to-all-start.1) | async-done | bytes 5242912 | tf_op jit(solution)/shard_map/all_to_all | solution.py:53
  113.0 300.3 %while.15 = (s32[]{:T(128)}, f32[1024,256]{1,0:T(8,128)S(1)}, f32[1024,256]{1,0:T(8,128)}, f32[1024,5,256]{2,0,1:T(8,128)}, f32[1024,5,256]{2,0,1:T(8,128)}, /*i...) while((s32[]{:T(128)}, f32[1024,256]{1,0:T(8,128)S(1)}, ...), condition=%wide.region_3.4_spmd, body=%wide.region_0.3_spmd.sunk | while | flops 58720264 | bytes 2360575 | solution.py:32
  114.2 16.8 %multiply_reduce_fusion.3 = (f32[64,256]{1,0:T(8,128)S(1)}, f32[64,256]{1,0:T(8,128)S(1)}) fusion(f32[64,256]{1,0:T(8,128)S(1)} %get-tuple-element.220, f32[64,256]{1,0:T(8,128)S(1)} %get-tuple-element.221, f32[64,256]{1,0:T(8,128)S(1)} %get-tuple-element.222, f32[64,256]{1,0:T(8,128)S(1)} %get-tuple-element.223, ...), kind=kLoop, calls=%fused_computation.2.clone.1 | loop fusion | flops 58687488 | bytes 786432 | tf_op jit(solution)/shard_map/while/body/eval_jaxpr/reduce_sum | solution.py:13
  133.0 16.8 %multiply_reduce_fusion.3 = (f32[64,256]{1,0:T(8,128)S(1)}, f32[64,256]{1,0:T(8,128)S(1)}) fusion(f32[64,256]{1,0:T(8,128)S(1)} %get-tuple-element.220, f32[64,256]{1,0:T(8,128)S(1)} %get-tuple-element.221, f32[64,256]{1,0:T(8,128)S(1)} %get-tuple-element.222, f32[64,256]{1,0:T(8,128)S(1)} %get-tuple-element.223, ...), kind=kLoop, calls=%fused_computation.2.clone.1 | loop fusion | flops 58687488 | bytes 786432 | tf_op jit(solution)/shard_map/while/body/eval_jaxpr/reduce_sum | solution.py:13
  151.7 16.8 %multiply_reduce_fusion.3 = (f32[64,256]{1,0:T(8,128)S(1)}, f32[64,256]{1,0:T(8,128)S(1)}) fusion(f32[64,256]{1,0:T(8,128)S(1)} %get-tuple-element.220, f32[64,256]{1,0:T(8,128)S(1)} %get-tuple-element.221, f32[64,256]{1,0:T(8,128)S(1)} %get-tuple-element.222, f32[64,256]{1,0:T(8,128)S(1)} %get-tuple-element.223, ...), kind=kLoop, calls=%fused_computation.2.clone.1 | loop fusion | flops 58687488 | bytes 786432 | tf_op jit(solution)/shard_map/while/body/eval_jaxpr/reduce_sum | solution.py:13
  170.5 16.8 %multiply_reduce_fusion.3 = (f32[64,256]{1,0:T(8,128)S(1)}, f32[64,256]{1,0:T(8,128)S(1)}) fusion(f32[64,256]{1,0:T(8,128)S(1)} %get-tuple-element.220, f32[64,256]{1,0:T(8,128)S(1)} %get-tuple-element.221, f32[64,256]{1,0:T(8,128)S(1)} %get-tuple-element.222, f32[64,256]{1,0:T(8,128)S(1)} %get-tuple-element.223, ...), kind=kLoop, calls=%fused_computation.2.clone.1 | loop fusion | flops 58687488 | bytes 786432 | tf_op jit(solution)/shard_map/while/body/eval_jaxpr/reduce_sum | solution.py:13
  189.3 16.8 %multiply_reduce_fusion.3 = (f32[64,256]{1,0:T(8,128)S(1)}, f32[64,256]{1,0:T(8,128)S(1)}) fusion(f32[64,256]{1,0:T(8,128)S(1)} %get-tuple-element.220, f32[64,256]{1,0:T(8,128)S(1)} %get-tuple-element.221, f32[64,256]{1,0:T(8,128)S(1)} %get-tuple-element.222, f32[64,256]{1,0:T(8,128)S(1)} %get-tuple-element.223, ...), kind=kLoop, calls=%fused_computation.2.clone.1 | loop fusion | flops 58687488 | bytes 786432 | tf_op jit(solution)/shard_map/while/body/eval_jaxpr/reduce_sum | solution.py:13
  208.0 16.8 %multiply_reduce_fusion.3 = (f32[64,256]{1,0:T(8,128)S(1)}, f32[64,256]{1,0:T(8,128)S(1)}) fusion(f32[64,256]{1,0:T(8,128)S(1)} %get-tuple-element.220, f32[64,256]{1,0:T(8,128)S(1)} %get-tuple-element.221, f32[64,256]{1,0:T(8,128)S(1)} %get-tuple-element.222, f32[64,256]{1,0:T(8,128)S(1)} %get-tuple-element.223, ...), kind=kLoop, calls=%fused_computation.2.clone.1 | loop fusion | flops 58687488 | bytes 786432 | tf_op jit(solution)/shard_map/while/body/eval_jaxpr/reduce_sum | solution.py:13
  226.8 16.8 %multiply_reduce_fusion.3 = (f32[64,256]{1,0:T(8,128)S(1)}, f32[64,256]{1,0:T(8,128)S(1)}) fusion(f32[64,256]{1,0:T(8,128)S(1)} %get-tuple-element.220, f32[64,256]{1,0:T(8,128)S(1)} %get-tuple-element.221, f32[64,256]{1,0:T(8,128)S(1)} %get-tuple-element.222, f32[64,256]{1,0:T(8,128)S(1)} %get-tuple-element.223, ...), kind=kLoop, calls=%fused_computation.2.clone.1 | loop fusion | flops 58687488 | bytes 786432 | tf_op jit(solution)/shard_map/while/body/eval_jaxpr/reduce_sum | solution.py:13
  245.6 16.8 %multiply_reduce_fusion.3 = (f32[64,256]{1,0:T(8,128)S(1)}, f32[64,256]{1,0:T(8,128)S(1)}) fusion(f32[64,256]{1,0:T(8,128)S(1)} %get-tuple-element.220, f32[64,256]{1,0:T(8,128)S(1)} %get-tuple-element.221, f32[64,256]{1,0:T(8,128)S(1)} %get-tuple-element.222, f32[64,256]{1,0:T(8,128)S(1)} %get-tuple-element.223, ...), kind=kLoop, calls=%fused_computation.2.clone.1 | loop fusion | flops 58687488 | bytes 786432 | tf_op jit(solution)/shard_map/while/body/eval_jaxpr/reduce_sum | solution.py:13
  264.4 16.8 %multiply_reduce_fusion.3 = (f32[64,256]{1,0:T(8,128)S(1)}, f32[64,256]{1,0:T(8,128)S(1)}) fusion(f32[64,256]{1,0:T(8,128)S(1)} %get-tuple-element.220, f32[64,256]{1,0:T(8,128)S(1)} %get-tuple-element.221, f32[64,256]{1,0:T(8,128)S(1)} %get-tuple-element.222, f32[64,256]{1,0:T(8,128)S(1)} %get-tuple-element.223, ...), kind=kLoop, calls=%fused_computation.2.clone.1 | loop fusion | flops 58687488 | bytes 786432 | tf_op jit(solution)/shard_map/while/body/eval_jaxpr/reduce_sum | solution.py:13
  283.1 16.8 %multiply_reduce_fusion.3 = (f32[64,256]{1,0:T(8,128)S(1)}, f32[64,256]{1,0:T(8,128)S(1)}) fusion(f32[64,256]{1,0:T(8,128)S(1)} %get-tuple-element.220, f32[64,256]{1,0:T(8,128)S(1)} %get-tuple-element.221, f32[64,256]{1,0:T(8,128)S(1)} %get-tuple-element.222, f32[64,256]{1,0:T(8,128)S(1)} %get-tuple-element.223, ...), kind=kLoop, calls=%fused_computation.2.clone.1 | loop fusion | flops 58687488 | bytes 786432 | tf_op jit(solution)/shard_map/while/body/eval_jaxpr/reduce_sum | solution.py:13
  301.9 16.8 %multiply_reduce_fusion.3 = (f32[64,256]{1,0:T(8,128)S(1)}, f32[64,256]{1,0:T(8,128)S(1)}) fusion(f32[64,256]{1,0:T(8,128)S(1)} %get-tuple-element.220, f32[64,256]{1,0:T(8,128)S(1)} %get-tuple-element.221, f32[64,256]{1,0:T(8,128)S(1)} %get-tuple-element.222, f32[64,256]{1,0:T(8,128)S(1)} %get-tuple-element.223, ...), kind=kLoop, calls=%fused_computation.2.clone.1 | loop fusion | flops 58687488 | bytes 786432 | tf_op jit(solution)/shard_map/while/body/eval_jaxpr/reduce_sum | solution.py:13
  320.6 16.8 %multiply_reduce_fusion.3 = (f32[64,256]{1,0:T(8,128)S(1)}, f32[64,256]{1,0:T(8,128)S(1)}) fusion(f32[64,256]{1,0:T(8,128)S(1)} %get-tuple-element.220, f32[64,256]{1,0:T(8,128)S(1)} %get-tuple-element.221, f32[64,256]{1,0:T(8,128)S(1)} %get-tuple-element.222, f32[64,256]{1,0:T(8,128)S(1)} %get-tuple-element.223, ...), kind=kLoop, calls=%fused_computation.2.clone.1 | loop fusion | flops 58687488 | bytes 786432 | tf_op jit(solution)/shard_map/while/body/eval_jaxpr/reduce_sum | solution.py:13
  339.4 16.8 %multiply_reduce_fusion.3 = (f32[64,256]{1,0:T(8,128)S(1)}, f32[64,256]{1,0:T(8,128)S(1)}) fusion(f32[64,256]{1,0:T(8,128)S(1)} %get-tuple-element.220, f32[64,256]{1,0:T(8,128)S(1)} %get-tuple-element.221, f32[64,256]{1,0:T(8,128)S(1)} %get-tuple-element.222, f32[64,256]{1,0:T(8,128)S(1)} %get-tuple-element.223, ...), kind=kLoop, calls=%fused_computation.2.clone.1 | loop fusion | flops 58687488 | bytes 786432 | tf_op jit(solution)/shard_map/while/body/eval_jaxpr/reduce_sum | solution.py:13
  358.2 16.8 %multiply_reduce_fusion.3 = (f32[64,256]{1,0:T(8,128)S(1)}, f32[64,256]{1,0:T(8,128)S(1)}) fusion(f32[64,256]{1,0:T(8,128)S(1)} %get-tuple-element.220, f32[64,256]{1,0:T(8,128)S(1)} %get-tuple-element.221, f32[64,256]{1,0:T(8,128)S(1)} %get-tuple-element.222, f32[64,256]{1,0:T(8,128)S(1)} %get-tuple-element.223, ...), kind=kLoop, calls=%fused_computation.2.clone.1 | loop fusion | flops 58687488 | bytes 786432 | tf_op jit(solution)/shard_map/while/body/eval_jaxpr/reduce_sum | solution.py:13
  376.9 16.8 %multiply_reduce_fusion.3 = (f32[64,256]{1,0:T(8,128)S(1)}, f32[64,256]{1,0:T(8,128)S(1)}) fusion(f32[64,256]{1,0:T(8,128)S(1)} %get-tuple-element.220, f32[64,256]{1,0:T(8,128)S(1)} %get-tuple-element.221, f32[64,256]{1,0:T(8,128)S(1)} %get-tuple-element.222, f32[64,256]{1,0:T(8,128)S(1)} %get-tuple-element.223, ...), kind=kLoop, calls=%fused_computation.2.clone.1 | loop fusion | flops 58687488 | bytes 786432 | tf_op jit(solution)/shard_map/while/body/eval_jaxpr/reduce_sum | solution.py:13
  395.7 16.8 %multiply_reduce_fusion.3 = (f32[64,256]{1,0:T(8,128)S(1)}, f32[64,256]{1,0:T(8,128)S(1)}) fusion(f32[64,256]{1,0:T(8,128)S(1)} %get-tuple-element.220, f32[64,256]{1,0:T(8,128)S(1)} %get-tuple-element.221, f32[64,256]{1,0:T(8,128)S(1)} %get-tuple-element.222, f32[64,256]{1,0:T(8,128)S(1)} %get-tuple-element.223, ...), kind=kLoop, calls=%fused_computation.2.clone.1 | loop fusion | flops 58687488 | bytes 786432 | tf_op jit(solution)/shard_map/while/body/eval_jaxpr/reduce_sum | solution.py:13
  418.9 15.6 %all-to-all-done.2 = f32[32,32,256]{2,1,0:T(8,128)S(1)} async-done(((f32[32,32,256]{2,1,0:T(8,128)}), f32[32,32,256]{2,1,0:T(8,128)S(1)}, u32[]{:S(2)}, u32[]{:S(2)}) %all-to-all-start.2) | async-done | bytes 1048608 | tf_op jit(solution)/shard_map/all_to_all | solution.py:61
  (74 shorter events, 58.5 us)
Async XLA Ops:
  1.5 15.5 %all-to-all-start = ((s32[32,1,32]{2,1,0:T(1,128)}), s32[32,1,32]{2,1,0:T(1,128)S(1)}, u32[]{:S(2)}, u32[]{:S(2)}) async-start(s32[32,1,32]{2,1,0:T(1,128)} %and_select_fusion), calls=%async_computation | async-start | bytes 32768 | tf_op jit(solution)/shard_map/all_to_all | solution.py:49
  35.6 70.6 %all-to-all-start.1 = ((f32[32,32,5,256]{3,1,2,0:T(8,128)}), f32[32,32,5,256]{3,1,2,0:T(8,128)}, u32[]{:S(2)}, u32[]{:S(2)}) async-start(f32[32,32,5,256]{3,1,2,0:T(8,128)} %copy.18), calls=%async_computation.1 | async-start | bytes 10485760 | tf_op jit(solution)/shard_map/all_to_all | solution.py:53
  51.1 7.5 %copy-start = (s32[1024,2]{0,1:T(2,128)S(1)}, s32[1024,2]{0,1:T(2,128)}, u32[]{:S(2)}) copy-start(s32[1024,2]{0,1:T(2,128)} %param.9) | copy-start | bytes 24580
  113.0 321.5 %copy-start.1 = (s32[16]{0:T(128)S(1)}, s32[16]{0:T(128)}, u32[]{:S(2)}) copy-start(s32[16]{0:T(128)} %param.8) | copy-start | bytes 196
  413.3 21.3 %all-to-all-start.2 = ((f32[32,32,256]{2,1,0:T(8,128)}), f32[32,32,256]{2,1,0:T(8,128)S(1)}, u32[]{:S(2)}, u32[]{:S(2)}) async-start(f32[32,32,256]{2,1,0:T(8,128)} %bitcast.17), calls=%async_computation.2 | async-start | bytes 2097152 | tf_op jit(solution)/shard_map/all_to_all | solution.py:61
where the time goes:
time: 438 us; the launch traced here: 436 us
  other arithmetic  284 us (65%)
  waiting for transfers between devices  68.9 us (16%)
  local copies, waits for them, and re-layouts  64.1 us (15%)
  starting transfers between devices  17 us (4%)
    reduce_sum x16, other arithmetic, pair_terms(): to_second = jnp.sum(kernel * mine[:, 0, :, None], axis=1)  269 us
    all_to_all x1, waiting for transfers between devices, local(): lax.all_to_all(served, 'frag', split_axis=0, concat_axis=0, tiled=True)  47.7 us
    mul x16, local copies, waits for them, and re-layouts, pair_terms(): to_first = jnp.sum(kernel * partner[:, 0, None, :], axis=2)  18.8 us
    gather x2, local copies, waits for them, and re-layouts, local(): served = packed[wanted]  18.4 us
    all_to_all x1, waiting for transfers between devices, local(): lax.all_to_all(to_second.reshape(peers, per_peer, width), 'frag', split_a...  15.6 us
    dynamic_update_slice x16, other arithmetic, one_block(): lax.dynamic_update_slice_in_dim(bufs[1], to_second * weight, start, 0)  11.2 us
    gather x1, local copies, waits for them, and re-layouts, local(): mine = packed[first_local]  10.6 us
  transfers between devices with their start and end apart: 3, of which 3 were waited for; matrix products, arithmetic and copies ran while one was open for 5% of the time, Pallas kernels for 0%

commit v1 on v0

v1 whole, which is shorter than its diff:
```python
import functools

import jax
import jax.numpy as jnp
from jax import lax
from jax.experimental import pallas as pl
from jax.experimental.pallas import tpu as pltpu
from jax.sharding import PartitionSpec as P

FRAG_DEV = 16
AUX = 256
ROWS = 96
NF = 64
NG = 128
CHUNK = 32
CPF = AUX // CHUNK
PER_TILE = 8
DUMMY = NF * AUX
DEPTH = 48
UNROLL = 8
WIDTH_FLOOR = 1.0 / 32.0


def pieces(value):
    first = value.astype(jnp.bfloat16).astype(jnp.float32)
    rest = value - first
    second = rest.astype(jnp.bfloat16).astype(jnp.float32)
    return first, second, rest - second


def pair_kernel(meta, *refs):
    packets = refs[:11]
    out_sib, out_far, out_near, out_own, outf_far, outf_near, outf_own = refs[11:18]
    (lhs, cfb, acc, acc_left, acc_right, rhs, cg, build, slots, counts, chunks, at_v, at_f, table_v, table, sem) = refs[18:]
    f_blocks = [packets[0], packets[1], packets[2], packets[3]]
    g_blocks = [packets[0]] + list(packets[4:])
    plane = meta[0]
    column = meta[1]

    def put_rows(r, value):
        for h in range(2):
            build[h, pl.ds(r * 16, 16), :] = value[:, 128 * h:128 * h + 128]

    def take_rows(h, at, count):
        return build.at[h][pl.ds(at, count, stride=16), :]

    lowest = None
    for i, blk in enumerate(f_blocks):
        x, y, z, w, c = (blk[pl.ds(16 * k, 16), :] for k in range(5))
        lowest = w if lowest is None else jnp.minimum(lowest, w)
        s = x * x + y * y + z * z + w
        one = jnp.ones_like(x)
        zero = jnp.zeros_like(x)
        px, py, pz = pieces(-2.0 * x), pieces(-2.0 * y), pieces(-2.0 * z)
        ps, pw, pc = pieces(s), pieces(w), pieces(c)
        for k in range(3):
            delta = one if k == 0 else zero
            extra = pc if k == 0 else (pw if k == 1 else (zero, zero, zero))
            rows = [px[k], py[k], pz[k], delta, ps[k], *extra,
                    px[k], py[k], pz[k], delta, px[k], py[k], pz[k], delta]
            for r, value in enumerate(rows):
                put_rows(16 * k + r, value)

        def one_row(lf, _, i=i):
            for h in range(2):
                start = pl.multiple_of((i * 16 + lf) * AUX + 128 * h, 128)
                lhs[pl.ds(start, 128), :] = take_rows(h, lf, DEPTH).T.astype(jnp.bfloat16)
            return 0

        lax.fori_loop(0, 16, one_row, 0, unroll=4)
    spare_lane = lax.broadcasted_iota(jnp.int32, (CHUNK, DEPTH), 1)
    lhs[pl.ds(DUMMY, CHUNK), :] = (spare_lane == 4).astype(jnp.float32).astype(jnp.bfloat16)

    pick = lax.broadcasted_iota(jnp.int32, (DEPTH, 128), 0)

    def spread(rows, lo, scale):
        sel = jnp.where((pick % 16 >= lo[0]) & (pick % 16 <= lo[1]) & (pick // 16 >= lo[2]) & (pick // 16 <= lo[3]), scale, 0.0)
        return jnp.dot(rows, sel.astype(jnp.bfloat16), preferred_element_type=jnp.float32)

    def one_spread(f, _):
        start = pl.multiple_of(f * AUX, AUX)
        cfb[pl.ds(start, AUX), :] = spread(lhs[pl.ds(start, AUX), :], (5, 7, 0, 0), 1.0)
        acc[pl.ds(start, AUX), :] = jnp.zeros((AUX, 128), jnp.float32)
        return 0

    lax.fori_loop(0, NF, one_spread, 0, unroll=4)
    cfb[pl.ds(DUMMY, CHUNK), :] = jnp.zeros((CHUNK, 128), jnp.float32)
    acc[pl.ds(DUMMY, CHUNK), :] = jnp.zeros((CHUNK, 128), jnp.float32)
    acc_left[...] = jnp.zeros_like(acc_left)
    acc_right[...] = jnp.zeros_like(acc_right)

    for j, blk in enumerate(g_blocks):
        x, y, z, w, c = (blk[pl.ds(16 * k, 16), :] for k in range(5))
        lowest = jnp.minimum(lowest, w)
        s = x * x + y * y + z * z + w
        one = jnp.ones_like(x)
        zero = jnp.zeros_like(x)
        px, py, pz, ps = pieces(x), pieces(y), pieces(z), pieces(s)
        rows = [px[0], py[0], pz[0], ps[0], one, zero, zero, zero,
                px[1], py[1], pz[1], ps[1], px[2], py[2], pz[2], ps[2]]
        for r, value in enumerate(rows):
            put_rows(r, value)
        cg[pl.ds(j * 16, 16), :] = c

        def one_column(lg, _, j=j):
            start = pl.multiple_of((j * 16 + lg) * 16, 16)
            rhs[pl.ds(start, 16), :] = jnp.concatenate([take_rows(h, lg, 16) for h in range(2)], axis=1).astype(jnp.bfloat16)
            return 0

        lax.fori_loop(0, 16, one_column, 0, unroll=8)

    lane = lax.broadcasted_iota(jnp.int32, (8, AUX), 1)
    back = jnp.zeros((8, AUX), jnp.float32)
    for j, blk in enumerate(g_blocks):
        shift = lax.rem(32 * j - 32 * column + 256, 256)
        turned = pltpu.roll(blk[pl.ds(80, 8), :], shift, 1)
        back = jnp.where(lane // 32 == j, turned, back)
    slots[...] = back
    g_lane = lax.broadcasted_iota(jnp.int32, (16, AUX), 0).astype(jnp.float32)
    g_ids = jnp.concatenate([g_lane + (16 * meta[8 + j]).astype(jnp.float32) for j in range(8)], axis=0)
    for i, blk in enumerate(f_blocks):
        f_ids = g_lane + (16 * meta[4 + i]).astype(jnp.float32)
        f_plane = meta[16 + i]

        def table_of(row_f, row_g):
            odd = (row_f + row_g) - 2.0 * jnp.floor((row_f + row_g) * 0.5)
            less = (row_f < row_g).astype(jnp.float32)
            use = (odd == less) & (row_f != row_g)
            row_f = jnp.where(use, row_f, -1.0)
            left = (row_f == f_ids).astype(jnp.float32).astype(jnp.bfloat16)
            right = (row_g == g_ids).astype(jnp.float32).astype(jnp.bfloat16)
            return lax.dot_general(left, right, (((1,), (1,)), ((), ())), preferred_element_type=jnp.float32)

        there = table_of(blk[pl.ds(80 + plane, 1), :], blk[pl.ds(84 + plane, 1), :])
        back_i = table_of(slots[pl.ds(4 + f_plane, 1), :], slots[pl.ds(f_plane, 1), :])
        counts[pl.ds(16 * i, 16), :] = there + back_i
        sizes = blk[pl.ds(88, 1), :]
        eye = lax.broadcasted_iota(jnp.int32, (16, AUX), 0) == lax.broadcasted_iota(jnp.int32, (16, AUX), 1)
        size_col = jnp.sum(jnp.where(eye, sizes, 0.0), axis=1, keepdims=True)
        many = jnp.floor((size_col + (CHUNK - 1)) * (1.0 / CHUNK))
        chunks[pl.ds(16 * i, 16), :] = jnp.broadcast_to(many, (16, 128))

    need = jnp.sum(counts[...] * chunks[...], axis=0, keepdims=True)
    rounds = ((jnp.max(need) + 127.0) * (1.0 / 128.0)).astype(jnp.int32)
    safe = jnp.min(lowest) >= WIDTH_FLOOR
    ones16 = lax.broadcasted_iota(jnp.int32, (128, 128), 0).astype(jnp.float32)

    def step(g, p, exact):
        entries = [pl.multiple_of(table[p + u, g], CHUNK) for u in range(PER_TILE)]
        block = rhs[pl.ds(pl.multiple_of(g * 16, 16), 16), :]
        left = jnp.concatenate([lhs[pl.ds(e, CHUNK), :] for e in entries], axis=0)
        if exact:
            at = pl.multiple_of(g * 16, 16)
            part = block.astype(jnp.float32)
            own = [part[k:k + 1] + part[8 + k:9 + k] + part[12 + k:13 + k] for k in range(3)]
            dist = None
            for k in range(3):
                mine = sum(jnp.dot(left, jnp.where((pick % 16 == k) & (pick // 16 < 3), -0.5, 0.0).astype(jnp.bfloat16), preferred_element_type=jnp.float32) for _ in range(1))
                mine = jnp.concatenate([mine, mine], axis=1)
                gap = mine - own[k]
                dist = gap * gap if dist is None else dist + gap * gap
            wide = spread(left, (5, 7, 1, 1), 1.0)
            dist = dist + jnp.concatenate([wide, wide], axis=1)
            dist = dist + wg_row(g)
            kern = lax.rsqrt(dist)
        else:
            right = jnp.concatenate([block, block, block], axis=0)
            kern = lax.rsqrt(jnp.dot(left, right, preferred_element_type=jnp.float32))
        k0, k1 = kern[:, :128], kern[:, 128:]
        weight = cg[pl.ds(g, 1), :]
        first = k0 * weight[:, :128] + k1 * weight[:, 128:]
        rows_c = jnp.concatenate([cfb[pl.ds(e, CHUNK), :] for e in entries], axis=0)
        sec0 = jnp.sum((k0 * rows_c).reshape(-1, 8, 128), axis=0)
        sec1 = jnp.sum((k1 * rows_c).reshape(-1, 8, 128), axis=0)
        base = pl.multiple_of(g * 8, 8)
        acc_left[pl.ds(base, 8), :] = acc_left[pl.ds(base, 8), :] + sec0
        acc_right[pl.ds(base, 8), :] = acc_right[pl.ds(base, 8), :] + sec1
        for u, e in enumerate(entries):
            acc[pl.ds(e, CHUNK), :] = acc[pl.ds(e, CHUNK), :] + first[u * CHUNK:(u + 1) * CHUNK]
        more = p + PER_TILE < table[136, g]
        g_next = jnp.where(more, g, g + 1)
        p_next = jnp.where(more, p + PER_TILE, 0)
        over = g_next > NG - 1
        return jnp.minimum(g_next, NG - 1), jnp.where(over, 128, p_next)

    def wg_row(g):
        j = g // 16
        lg = g % 16
        row = jnp.zeros((1, AUX), jnp.float32)
        for k, blk in enumerate(g_blocks):
            row = jnp.where(j == k, blk[pl.ds(48 + lg, 1), :], row)
        return row

    def one_round(r, _):
        at_v[...] = ones16 + (128 * r).astype(jnp.float32)
        at = at_v[...]

        def scan(f, state):
            code, begin, total = state
            many = chunks[pl.ds(f, 1), :]
            hit = at >= total
            code = jnp.where(hit, f.astype(jnp.float32) * 16.0 + many, code)
            begin = jnp.where(hit, total, begin)
            return code, begin, total + counts[pl.ds(f, 1), :] * many

        at_f[...] = jnp.zeros((128, 128), jnp.float32)
        flat = at_f[...]
        code, begin, total = lax.fori_loop(0, NF, scan, (flat, flat, flat[0:1]), unroll=4)
        frag = jnp.floor(code * (1.0 / 16.0))
        many = code - 16.0 * frag
        offset = at - begin
        offset = offset - many * jnp.floor((offset + 0.5) / many)
        entry = (frag * CPF + offset) * CHUNK
        entry = jnp.where(at < total, entry, float(DUMMY))
        table_v[pl.ds(0, 128), :] = entry.astype(jnp.int32)
        table_v[pl.ds(128, 8), :] = jnp.full((8, 128), DUMMY, jnp.int32)
        left_over = jnp.clip(total - (128 * r).astype(jnp.float32), 0.0, 128.0)
        tiles = jnp.maximum(jnp.floor((left_over + (PER_TILE - 1)) * (1.0 / PER_TILE)), 1.0)
        tile_sum = jnp.sum(tiles, axis=1, keepdims=True)
        row8 = lax.broadcasted_iota(jnp.int32, (8, 128), 0)
        table_v[pl.ds(136, 8), :] = jnp.where(row8 == 0, left_over, tile_sum).astype(jnp.int32)
        copy = pltpu.make_async_copy(table_v, table, sem)
        copy.start()
        copy.wait()
        total_tiles = table[137, 0]

        def many_tiles(exact, width):
            def body(_, state):
                for _u in range(width):
                    state = step(*state, exact)
                return state

            lax.fori_loop(0, (total_tiles + (width - 1)) // width, body, (jnp.int32(0), jnp.int32(0)))

        @pl.when(safe)
        def _():
            many_tiles(False, UNROLL)

        @pl.when(jnp.logical_not(safe))
        def _():
            many_tiles(True, 1)

        return 0

    lax.fori_loop(0, rounds, one_round, 0)

    lanes = lax.broadcasted_iota(jnp.int32, (AUX, 128), 1)

    def collect(f, out):
        start = pl.multiple_of(f * AUX, AUX)
        col = jnp.sum(acc[pl.ds(start, AUX), :], axis=1, keepdims=True)
        return jnp.where(lanes == f, col, out)

    rows_out = lax.fori_loop(0, NF, collect, acc[pl.ds(DUMMY - AUX, AUX), :]).T
    outf_own[...] = rows_out[0:16]
    outf_near[...] = rows_out[16:32]
    outf_far[...] = rows_out[32:64]
    cols = []
    for part in (acc_left, acc_right):
        half = part[pl.ds(0, NG, stride=8), :]
        for r in range(1, 8):
            half = half + part[pl.ds(r, NG, stride=8), :]
        cols.append(half)
    cols = jnp.concatenate(cols, axis=1)
    out_own[...] = cols[0:16]
    out_near[...] = cols[16:32]
    out_far[...] = cols[32:64]
    out_sib[...] = cols[64:128]


def rectangle(meta, packets):
    vmem = pl.BlockSpec(memory_space=pltpu.VMEM)
    shape = lambda rows: jax.ShapeDtypeStruct((rows, AUX), jnp.float32)
    return pl.pallas_call(
        pair_kernel,
        out_shape=(shape(64), shape(32), shape(16), shape(16), shape(32), shape(16), shape(16)),
        in_specs=[pl.BlockSpec(memory_space=pltpu.SMEM)] + [vmem] * 11,
        out_specs=(vmem,) * 7,
        scratch_shapes=[
            pltpu.VMEM((DUMMY + CHUNK, DEPTH), jnp.bfloat16),
            pltpu.VMEM((DUMMY + CHUNK, 128), jnp.float32),
            pltpu.VMEM((DUMMY + CHUNK, 128), jnp.float32),
            pltpu.VMEM((NG * 8, 128), jnp.float32),
            pltpu.VMEM((NG * 8, 128), jnp.float32),
            pltpu.VMEM((NG * 16, AUX), jnp.bfloat16),
            pltpu.VMEM((NG, AUX), jnp.float32),
            pltpu.VMEM((2, DEPTH * 16, 128), jnp.float32),
            pltpu.VMEM((8, AUX), jnp.float32),
            pltpu.VMEM((NF, 128), jnp.float32),
            pltpu.VMEM((NF, 128), jnp.float32),
            pltpu.VMEM((128, 128), jnp.float32),
            pltpu.VMEM((128, 128), jnp.float32),
            pltpu.VMEM((144, 128), jnp.int32),
            pltpu.SMEM((144, 128), jnp.int32),
            pltpu.SemaphoreType.DMA,
        ],
        compiler_params=pltpu.CompilerParams(vmem_limit_bytes=56 * 2**20),
    )(meta, *packets)


def index_of(z, x, c):
    return (z * 4 + x) * 2 + c


def partners(move):
    return [
        (index_of(z, x, c), index_of(*move(z, x, c)))
        for z in range(4) for x in range(4) for c in range(2)
    ]


X_NEAR = partners(lambda z, x, c: (z, x ^ 1, c))
X_FAR = partners(lambda z, x, c: (z, 3 - x, c))
Z_NEAR = partners(lambda z, x, c: (z ^ 1, x, c))
Z_FAR = partners(lambda z, x, c: (3 - z, x, c))
CORE = partners(lambda z, x, c: (z, x, c ^ 1))


def swap(array, pairs):
    return lax.ppermute(array, "frag", pairs)


def local(coeffs, centres, frag_sizes, pairs):
    me = lax.axis_index("frag")
    z, x, c = me // 8, (me // 2) % 4, me % 2
    mask = (jnp.arange(AUX, dtype=jnp.int32)[None, :] < frag_sizes[:, None]).astype(jnp.float32)
    packet = jnp.concatenate(
        [
            centres.transpose(1, 0, 2).reshape(4 * FRAG_DEV, AUX),
            coeffs * mask,
            pairs.T.reshape(8, AUX).astype(jnp.float32),
            jnp.pad(frag_sizes.astype(jnp.float32)[None, :], ((0, 7), (0, AUX - FRAG_DEV))),
        ],
        axis=0,
    )
    zs = jnp.stack([z, z ^ 1, 3 - z, (3 - z) ^ 1])
    xs = jnp.stack([x, x ^ 1, 3 - x, (3 - x) ^ 1])
    f_dev = index_of(zs, x, c)
    g_dev = jnp.concatenate([index_of(z, xs, c), index_of(z, xs, c ^ 1)])
    zero = jnp.zeros((2,), jnp.int32)
    meta = jnp.concatenate([jnp.stack([z, 2 * x + c]), zero, f_dev, g_dev, zs]).astype(jnp.int32)

    x_near = swap(packet, X_NEAR)
    z_near = swap(packet, Z_NEAR)
    x_far = swap(packet, X_FAR)
    z_far = swap(packet, Z_FAR)
    x_last = swap(x_near, X_FAR)
    z_last = swap(z_near, Z_FAR)
    own_c = swap(packet, CORE)
    near_c = swap(x_near, CORE)
    far_c = swap(x_far, CORE)
    last_c = swap(x_last, CORE)

    g_sib, g_far, g_near, g_own, f_far, f_near, f_own = rectangle(
        meta,
        (packet, z_near, z_far, z_last, x_near, x_far, x_last, own_c, near_c, far_c, last_c),
    )
    f_back = swap(f_far, Z_FAR)
    sib_back = swap(g_sib, CORE)
    far_back = swap(g_far + sib_back[32:], X_FAR)
    f_last = swap(f_near + f_back[16:], Z_NEAR)
    near_back = swap(g_near + sib_back[16:32] + far_back[16:], X_NEAR)
    total = f_own + f_back[:16] + f_last + g_own + sib_back[:16] + far_back[:16] + near_back
    return total * mask


def solution(mesh):
    return jax.shard_map(
        local,
        mesh=mesh,
        in_specs=(
            P(("cplx", "frag"), None),
            P(("cplx", "frag"), None, None),
            P(("cplx", "frag")),
            P(("cplx", "frag"), None),
        ),
        out_specs=P(("cplx", "frag"), None),
        check_vma=False,
    )
```

time: 438 us -> 196 us (0.45)
  other arithmetic: 284 us -> 3.81 us
  Pallas kernels: 0 us -> 155 us
  local copies, waits for them, and re-layouts: 64.1 us -> 2.52 us
  waiting for transfers between devices: 68.9 us -> 15.6 us
    reduce_sum x16 -> x0, other arithmetic: 269 us -> none  [pair_terms(): to_second = jnp.sum(kernel * mine[:, 0, :, None], axis=1)]
    pallas_call x0 -> x1, Pallas kernels: none -> 155 us  [rectangle(): pl.pallas_call(pair_kernel, out_shape=(shape(64), shape(32), shape(16), s...]
    all_to_all x3 -> x0, waiting for transfers between devices: 68.9 us -> none  [the longest x1 47.7 us: local(): lax.all_to_all(served, 'frag', split_axis=0, concat_axis=0, tiled=True)]
    gather x3 -> x0, local copies, waits for them, and re-layouts: 29 us -> none  [the longest x2 18.4 us: local(): served = packed[wanted]]
    mul x16 -> x0, local copies, waits for them, and re-layouts: 18.8 us -> none  [pair_terms(): to_first = jnp.sum(kernel * partner[:, 0, None, :], axis=2)]
    all_to_all x3 -> x0, starting transfers between devices: 17 us -> none  [the longest x1 8.25 us: local(): lax.all_to_all(second_slot.reshape(peers, per_peer), 'frag', split_axis=0...]
    ppermute x0 -> x15, starting transfers between devices: none -> 15.7 us  [swap(): return lax.ppermute(array, 'frag', pairs)]
    ppermute x0 -> x15, waiting for transfers between devices: none -> 15.6 us  [swap(): return lax.ppermute(array, 'frag', pairs)]
  transfers between devices with their start and end apart: 3 -> 15, of which waited for: 3 -> 7; matrix products, arithmetic and copies ran while one was open for 5% -> 1% of each run, Pallas kernels for 0% -> 0%
where the time goes in v1:
time: 196 us; the launch traced here: 193 us
  Pallas kernels  155 us (79%)
  starting transfers between devices  15.7 us (8%)
  waiting for transfers between devices  15.6 us (8%)
  other arithmetic  3.81 us (2%)
  local copies, waits for them, and re-layouts  2.52 us (1%)
    pallas_call x1, Pallas kernels, rectangle(): pl.pallas_call(pair_kernel, out_shape=(shape(64), shape(32), shape(16), s...  155 us
    ppermute x15, starting transfers between devices, swap(): return lax.ppermute(array, 'frag', pairs)  15.7 us
    ppermute x15, waiting for transfers between devices, swap(): return lax.ppermute(array, 'frag', pairs)  15.6 us
  transfers between devices with their start and end apart: 15, of which 7 were waited for; matrix products, arithmetic and copies ran while one was open for 1% of the time, Pallas kernels for 0%

profile of v1, /device:TPU:0, one launch (start us, length us, event | category | flops | bytes accessed | tf_op | source)
XLA Modules:
  0.0 192.8 jit_solution(2522266620914189058)
XLA Ops:
  0.0 0.7 convert_bitcast_fusion.1
  0.7 0.7 convert_bitcast_fusion
  1.4 0.8 fusion.4
  2.2 1.7 collective-permute-start.3
  3.9 2.1 %collective-permute-start.4 = (f32[96,256]{1,0:T(8,128)S(1)}, f32[96,256]{1,0:T(8,128)S(1)}, u32[]{:S(2)}, u32[]{:S(2)}) collective-permute-start(f32[96,256]{1,0:T(8,128)S(1)} %select_maximum_fusion.refs_0_), channel_id=1, source_target_pairs={{0,6},{1,7},{2,4},{3,5},{4,2},{5,3},{6,0},{7,1},{8,14},{9,15},{10,... | collective-permute-start | bytes 294920 | tf_op jit(solution)/shard_map/ppermute | solution.py:320
  6.0 4.0 %collective-permute-start.1 = (f32[96,256]{1,0:T(8,128)S(1)}, f32[96,256]{1,0:T(8,128)S(1)}, u32[]{:S(2)}, u32[]{:S(2)}) collective-permute-start(f32[96,256]{1,0:T(8,128)S(1)} %select_maximum_fusion.refs_0_), channel_id=1, source_target_pairs={{0,24},{1,25},{2,26},{3,27},{4,28},{5,29},{6,30},{7,31},{8,16},{9,... | collective-permute-start | bytes 294920 | tf_op jit(solution)/shard_map/ppermute | solution.py:320
  10.0 1.2 collective-permute-start.5
  12.0 2.7 %collective-permute-done.refs_1_ = f32[96,256]{1,0:T(8,128)S(1)} collective-permute-done((f32[96,256]{1,0:T(8,128)S(1)}, f32[96,256]{1,0:T(8,128)S(1)}, u32[]{:S(2)}, u32[]{:S(2)}) %collective-permute-start) | collective-permute-done | bytes 98336 | tf_op jit(solution)/shard_map/ppermute | solution.py:320
  15.0 1.0 collective-permute-done.5.refs_6_
  16.1 0.6 concatenate.7.meta
  16.7 3.8 %collective-permute-done.2.refs_3_ = f32[96,256]{1,0:T(8,128)S(1)} collective-permute-done((f32[96,256]{1,0:T(8,128)S(1)}, f32[96,256]{1,0:T(8,128)S(1)}, u32[]{:S(2)}, u32[]{:S(2)}) %collective-permute-start.2) | collective-permute-done | bytes 98336 | tf_op jit(solution)/shard_map/ppermute | solution.py:320
  20.6 0.5 copy-done.9
  21.1 0.6 copy-done.10
  21.8 155.0 %shard_map.46 = (f32[64,256]{1,0:T(8,128)}, f32[32,256]{1,0:T(8,128)}, f32[16,256]{1,0:T(8,128)}, f32[16,256]{1,0:T(8,128)}, f32[32,256]{1,0:T(8,128)}, /*index=5*/f32[16,256]{1,0:T(8,128)}, f32[16,256]{1,0:T(8,128)}) custom-call(s32[20]{0:T(128)} %concatenate.7.meta, f32[96,256]{1,0:T(8,128)} %copy-done, f32[96,256]{1,0:T(8,128)} %copy-done.5, ...), custom_call_target="tpu_custom_call" | custom-call | tf_op jit(solution)/shard_map/pallas_call | solution.py:274
  176.8 2.7 %collective-permute-start.12 = (f32[64,256]{1,0:T(8,128)}, f32[64,256]{1,0:T(8,128)S(1)}, u32[]{:S(2)}, u32[]{:S(2)}) collective-permute-start(f32[64,256]{1,0:T(8,128)} %get-tuple-element.16), channel_id=1, source_target_pairs={{0,1},{1,0},{2,3},{3,2},{4,5},{5,4},{6,7},{7,6},{8,9},{9,8},{10,11... | collective-permute-start | bytes 196616 | tf_op jit(solution)/shard_map/ppermute | solution.py:320
  179.5 2.2 %collective-permute-start.10 = (f32[32,256]{1,0:T(8,128)}, f32[32,256]{1,0:T(8,128)S(1)}, u32[]{:S(2)}, u32[]{:S(2)}) collective-permute-start(f32[32,256]{1,0:T(8,128)} %get-tuple-element.13), channel_id=1, source_target_pairs={{0,24},{1,25},{2,26},{3,27},{4,28},{5,29},{6,30},{7,31},{8,16},{9,... | collective-permute-start | bytes 98312 | tf_op jit(solution)/shard_map/ppermute | solution.py:320
  181.8 0.8 slice_add_fusion
  182.5 2.3 %collective-permute-done.10 = f32[32,256]{1,0:T(8,128)S(1)} collective-permute-done((f32[32,256]{1,0:T(8,128)}, f32[32,256]{1,0:T(8,128)S(1)}, u32[]{:S(2)}, u32[]{:S(2)}) %collective-permute-start.10) | collective-permute-done | bytes 32800 | tf_op jit(solution)/shard_map/ppermute | solution.py:320
  184.9 0.8 collective-permute-start.11
  185.7 2.0 %collective-permute-done.13 = f32[32,256]{1,0:T(8,128)S(1)} collective-permute-done((f32[32,256]{1,0:T(8,128)S(1)}, f32[32,256]{1,0:T(8,128)S(1)}, u32[]{:S(2)}, u32[]{:S(2)}) %collective-permute-start.13) | collective-permute-done | bytes 32800 | tf_op jit(solution)/shard_map/ppermute | solution.py:320
  187.8 0.9 collective-permute-done.11
  188.7 2.8 %collective-permute-done.14 = f32[16,256]{1,0:T(8,128)S(1)} collective-permute-done((f32[16,256]{1,0:T(8,128)S(1)}, f32[16,256]{1,0:T(8,128)S(1)}, u32[]{:S(2)}, u32[]{:S(2)}) %collective-permute-start.14) | collective-permute-done | bytes 16416 | tf_op jit(solution)/shard_map/ppermute | solution.py:320
  191.5 0.6 copy-done.16
  192.2 0.7 fusion.1
  (55 shorter events, 1.2 us)
Async XLA Ops:
  2.2 18.3 %copy-start = (f32[96,256]{1,0:T(8,128)}, f32[96,256]{1,0:T(8,128)S(1)}, u32[]{:S(2)}) copy-start(f32[96,256]{1,0:T(8,128)S(1)} %select_maximum_fusion.refs_0_) | copy-start | bytes 294916
  2.2 7.8 %collective-permute-start.3 = (f32[96,256]{1,0:T(8,128)S(1)}, f32[96,256]{1,0:T(8,128)S(1)}, u32[]{:S(2)}, u32[]{:S(2)}) collective-permute-start(f32[96,256]{1,0:T(8,128)S(1)} %select_maximum_fusion.refs_0_), channel_id=1, source_target_pairs={{0,2},{1,3},{2,0},{3,1},{4,6},{5,7},{6,4},{7,5},{8,10},{9,11},{10,... | collective-permute-start | bytes 294920 | tf_op jit(solution)/shard_map/ppermute | solution.py:320
  3.9 7.5 %collective-permute-start.6 = (f32[96,256]{1,0:T(8,128)S(1)}, f32[96,256]{1,0:T(8,128)S(1)}, u32[]{:S(2)}, u32[]{:S(2)}) collective-permute-start(f32[96,256]{1,0:T(8,128)S(1)} %select_maximum_fusion.refs_0_), channel_id=1, source_target_pairs={{0,1},{1,0},{2,3},{3,2},{4,5},{5,4},{6,7},{7,6},{8,9},{9,8},{10,11... | collective-permute-start | bytes 294920 | tf_op jit(solution)/shard_map/ppermute | solution.py:320
  3.9 7.5 %collective-permute-start.4 = (f32[96,256]{1,0:T(8,128)S(1)}, f32[96,256]{1,0:T(8,128)S(1)}, u32[]{:S(2)}, u32[]{:S(2)}) collective-permute-start(f32[96,256]{1,0:T(8,128)S(1)} %select_maximum_fusion.refs_0_), channel_id=1, source_target_pairs={{0,6},{1,7},{2,4},{3,5},{4,2},{5,3},{6,0},{7,1},{8,14},{9,15},{10,... | collective-permute-start | bytes 294920 | tf_op jit(solution)/shard_map/ppermute | solution.py:320
  6.0 10.7 %collective-permute-start.1 = (f32[96,256]{1,0:T(8,128)S(1)}, f32[96,256]{1,0:T(8,128)S(1)}, u32[]{:S(2)}, u32[]{:S(2)}) collective-permute-start(f32[96,256]{1,0:T(8,128)S(1)} %select_maximum_fusion.refs_0_), channel_id=1, source_target_pairs={{0,24},{1,25},{2,26},{3,27},{4,28},{5,29},{6,30},{7,31},{8,16},{9,... | collective-permute-start | bytes 294920 | tf_op jit(solution)/shard_map/ppermute | solution.py:320
  10.0 4.6 %collective-permute-start = (f32[96,256]{1,0:T(8,128)S(1)}, f32[96,256]{1,0:T(8,128)S(1)}, u32[]{:S(2)}, u32[]{:S(2)}) collective-permute-start(f32[96,256]{1,0:T(8,128)S(1)} %select_maximum_fusion.refs_0_), channel_id=1, source_target_pairs={{0,8},{1,9},{2,10},{3,11},{4,12},{5,13},{6,14},{7,15},{8,0},{9,1},... | collective-permute-start | bytes 294920 | tf_op jit(solution)/shard_map/ppermute | solution.py:320
  10.0 10.5 %copy-start.1 = (f32[96,256]{1,0:T(8,128)}, f32[96,256]{1,0:T(8,128)S(1)}, u32[]{:S(2)}) copy-start(f32[96,256]{1,0:T(8,128)S(1)} %collective-permute-done.3.refs_4_) | copy-start | bytes 294916
  10.0 5.9 %collective-permute-start.5 = (f32[96,256]{1,0:T(8,128)S(1)}, f32[96,256]{1,0:T(8,128)S(1)}, u32[]{:S(2)}, u32[]{:S(2)}) collective-permute-start(f32[96,256]{1,0:T(8,128)S(1)} %collective-permute-done.3.refs_4_), channel_id=1, source_target_pairs={{0,6},{1,7},{2,4},{3,5},{4,2},{5,3},{6,0},{7,1},{8,14},{9,15},{10,... | collective-permute-start | bytes 294920 | tf_op jit(solution)/shard_map/ppermute | solution.py:320
  11.4 9.2 %copy-start.2 = (f32[96,256]{1,0:T(8,128)}, f32[96,256]{1,0:T(8,128)S(1)}, u32[]{:S(2)}) copy-start(f32[96,256]{1,0:T(8,128)S(1)} %collective-permute-done.6.refs_7_) | copy-start | bytes 294916
  11.4 5.4 %collective-permute-start.7 = (f32[96,256]{1,0:T(8,128)S(1)}, f32[96,256]{1,0:T(8,128)S(1)}, u32[]{:S(2)}, u32[]{:S(2)}) collective-permute-start(f32[96,256]{1,0:T(8,128)S(1)} %collective-permute-done.3.refs_4_), channel_id=1, source_target_pairs={{0,1},{1,0},{2,3},{3,2},{4,5},{5,4},{6,7},{7,6},{8,9},{9,8},{10,11... | collective-permute-start | bytes 294920 | tf_op jit(solution)/shard_map/ppermute | solution.py:320
  11.5 9.1 %copy-start.3 = (f32[96,256]{1,0:T(8,128)}, f32[96,256]{1,0:T(8,128)S(1)}, u32[]{:S(2)}) copy-start(f32[96,256]{1,0:T(8,128)S(1)} %collective-permute-done.4.refs_5_) | copy-start | bytes 294916
  11.5 5.2 %collective-permute-start.8 = (f32[96,256]{1,0:T(8,128)S(1)}, f32[96,256]{1,0:T(8,128)S(1)}, u32[]{:S(2)}, u32[]{:S(2)}) collective-permute-start(f32[96,256]{1,0:T(8,128)S(1)} %collective-permute-done.4.refs_5_), channel_id=1, source_target_pairs={{0,1},{1,0},{2,3},{3,2},{4,5},{5,4},{6,7},{7,6},{8,9},{9,8},{10,11... | collective-permute-start | bytes 294920 | tf_op jit(solution)/shard_map/ppermute | solution.py:320
  14.7 5.9 %copy-start.5 = (f32[96,256]{1,0:T(8,128)}, f32[96,256]{1,0:T(8,128)S(1)}, u32[]{:S(2)}) copy-start(f32[96,256]{1,0:T(8,128)S(1)} %collective-permute-done.refs_1_) | copy-start | bytes 294916
  14.7 5.8 %collective-permute-start.2 = (f32[96,256]{1,0:T(8,128)S(1)}, f32[96,256]{1,0:T(8,128)S(1)}, u32[]{:S(2)}, u32[]{:S(2)}) collective-permute-start(f32[96,256]{1,0:T(8,128)S(1)} %collective-permute-done.refs_1_), channel_id=1, source_target_pairs={{0,24},{1,25},{2,26},{3,27},{4,28},{5,29},{6,30},{7,31},{8,16},{9,... | collective-permute-start | bytes 294920 | tf_op jit(solution)/shard_map/ppermute | solution.py:320
  16.0 4.6 %copy-start.6 = (f32[96,256]{1,0:T(8,128)}, f32[96,256]{1,0:T(8,128)S(1)}, u32[]{:S(2)}) copy-start(f32[96,256]{1,0:T(8,128)S(1)} %collective-permute-done.5.refs_6_) | copy-start | bytes 294916
  16.0 4.5 %collective-permute-start.9 = (f32[96,256]{1,0:T(8,128)S(1)}, f32[96,256]{1,0:T(8,128)S(1)}, u32[]{:S(2)}, u32[]{:S(2)}) collective-permute-start(f32[96,256]{1,0:T(8,128)S(1)} %collective-permute-done.5.refs_6_), channel_id=1, source_target_pairs={{0,1},{1,0},{2,3},{3,2},{4,5},{5,4},{6,7},{7,6},{8,9},{9,8},{10,11... | collective-permute-start | bytes 294920 | tf_op jit(solution)/shard_map/ppermute | solution.py:320
  16.7 3.9 %copy-start.4 = (f32[96,256]{1,0:T(8,128)}, f32[96,256]{1,0:T(8,128)S(1)}, u32[]{:S(2)}) copy-start(f32[96,256]{1,0:T(8,128)S(1)} %collective-permute-done.1.refs_2_) | copy-start | bytes 294916
  16.7 3.9 %copy-start.8 = (f32[96,256]{1,0:T(8,128)}, f32[96,256]{1,0:T(8,128)S(1)}, u32[]{:S(2)}) copy-start(f32[96,256]{1,0:T(8,128)S(1)} %collective-permute-done.8.refs_9_) | copy-start | bytes 294916
  16.7 3.9 %copy-start.7 = (f32[96,256]{1,0:T(8,128)}, f32[96,256]{1,0:T(8,128)S(1)}, u32[]{:S(2)}) copy-start(f32[96,256]{1,0:T(8,128)S(1)} %collective-permute-done.7.refs_8_) | copy-start | bytes 294916
  176.8 5.0 %collective-permute-start.12 = (f32[64,256]{1,0:T(8,128)}, f32[64,256]{1,0:T(8,128)S(1)}, u32[]{:S(2)}, u32[]{:S(2)}) collective-permute-start(f32[64,256]{1,0:T(8,128)} %get-tuple-element.16), channel_id=1, source_target_pairs={{0,1},{1,0},{2,3},{3,2},{4,5},{5,4},{6,7},{7,6},{8,9},{9,8},{10,11... | collective-permute-start | bytes 196616 | tf_op jit(solution)/shard_map/ppermute | solution.py:320
  179.5 5.3 %collective-permute-start.10 = (f32[32,256]{1,0:T(8,128)}, f32[32,256]{1,0:T(8,128)S(1)}, u32[]{:S(2)}, u32[]{:S(2)}) collective-permute-start(f32[32,256]{1,0:T(8,128)} %get-tuple-element.13), channel_id=1, source_target_pairs={{0,24},{1,25},{2,26},{3,27},{4,28},{5,29},{6,30},{7,31},{8,16},{9,... | collective-permute-start | bytes 98312 | tf_op jit(solution)/shard_map/ppermute | solution.py:320
  182.5 5.1 %collective-permute-start.13 = (f32[32,256]{1,0:T(8,128)S(1)}, f32[32,256]{1,0:T(8,128)S(1)}, u32[]{:S(2)}, u32[]{:S(2)}) collective-permute-start(f32[32,256]{1,0:T(8,128)S(1)} %slice_add_fusion), channel_id=1, source_target_pairs={{0,6},{1,7},{2,4},{3,5},{4,2},{5,3},{6,0},{7,1},{8,14},{9,15},{10,... | collective-permute-start | bytes 98312 | tf_op jit(solution)/shard_map/ppermute | solution.py:320
  184.9 3.8 %collective-permute-start.11 = (f32[16,256]{1,0:T(8,128)S(1)}, f32[16,256]{1,0:T(8,128)S(1)}, u32[]{:S(2)}, u32[]{:S(2)}) collective-permute-start(f32[16,256]{1,0:T(8,128)S(1)} %slice_add_fusion.5), channel_id=1, source_target_pairs={{0,8},{1,9},{2,10},{3,11},{4,12},{5,13},{6,14},{7,15},{8,0},{9,1},... | collective-permute-start | bytes 49160 | tf_op jit(solution)/shard_map/ppermute | solution.py:320
  187.7 3.8 %collective-permute-start.14 = (f32[16,256]{1,0:T(8,128)S(1)}, f32[16,256]{1,0:T(8,128)S(1)}, u32[]{:S(2)}, u32[]{:S(2)}) collective-permute-start(f32[16,256]{1,0:T(8,128)S(1)} %slice_add_fusion.1), channel_id=1, source_target_pairs={{0,2},{1,3},{2,0},{3,1},{4,6},{5,7},{6,4},{7,5},{8,10},{9,11},{10,... | collective-permute-start | bytes 49160 | tf_op jit(solution)/shard_map/ppermute | solution.py:320
  (8 other events, 17.7 us)
